TPU v7x, 32 devices: a whole 2x2x4 slice. The times are simulated.
32 devices in a mesh: row: 16 (over z, y, x), col: 2 (over core).
Axes of the slice: x: 2, y: 2, z: 4, core: 2. Of those that a mesh axis runs over, the one named last changes fastest.
Arguments:
- token_keys: bfloat16 [16384, 768], P(('row', 'col')), may hold values from -6 to 6
- token_values: bfloat16 [16384, 768], P(('row', 'col')), may hold values from -6 to 6
- token_queries: bfloat16 [16384, 768], P(('row', 'col')), may hold values from -6 to 6
- step_rates: float32 [16384], P(('row', 'col')), may hold values from 5e-05 to 0.0005
- fast_gate: float32 [768, 768], P('col'), may hold values from -0.21875 to 0.21875
- fast_up: float32 [768, 768], P('col'), may hold values from -0.21875 to 0.21875
- fast_down: float32 [768, 768], P('col'), may hold values from -0.21875 to 0.21875
- norm_gain: float32 [768], replicated, may hold values from 0.25 to 1.75
- proj_query: bfloat16 [768, 768], replicated, may hold values from -0.21875 to 0.21875
- proj_key: bfloat16 [768, 768], replicated, may hold values from -0.21875 to 0.21875
- proj_value: bfloat16 [768, 768], replicated, may hold values from -0.21875 to 0.21875
- head_temper: float32 [12], replicated, may hold values from 1 to 12
Outputs:
- attended: bfloat16 [16384, 768], P(('row', 'col'))
- new_gate: float32 [768, 768], P('col')
- new_up: float32 [768, 768], P('col')
- new_down: float32 [768, 768], P('col')
All inputs are finite; a program needn't handle non-finite values.
Results may differ from a plain program's by a relative error of at most 0.035.
The roundings to bfloat16 on the way count: a program that leaves them out, or rounds other values in their place, can miss the bound.
Values may be sent and summed in bfloat16 or wider, within the bound.
A program may use at most 64 MiB of HBM per device.

v0:
```python
import math

import jax
import jax.numpy as jnp
from jax import lax
from jax.sharding import PartitionSpec as P

EPS_NORM = 1e-06


def padded_2(cells, sides, width):
    for axis, dim in sides:
        count = lax.axis_size(axis)
        head = lax.slice_in_dim(cells, 0, width, axis=dim)
        tail = lax.slice_in_dim(cells, cells.shape[dim] - width, cells.shape[dim], axis=dim)
        cells = jnp.concatenate(
            [
                lax.ppermute(tail, axis, [(i, (i + 1) % count) for i in range(count)]),
                cells,
                lax.ppermute(head, axis, [((i + 1) % count, i) for i in range(count)]),
            ],
            axis=dim,
        )
    return cells


def dot_rows(left, right):
    return lax.dot_general(
        left, right, (((1,), (1,)), ((), ())), preferred_element_type=jnp.float32
    )


def dot_cols(left, right):
    return lax.dot_general(
        left, right, (((0,), (0,)), ((), ())), preferred_element_type=jnp.float32
    )


def fast_gradients(token_keys, token_values, step_rates, gate_b, up_b, down_b):
    pre_gate = dot_rows(token_keys, gate_b)
    pre_up = dot_rows(token_keys, up_b)
    sigmoid_gate = jax.nn.sigmoid(pre_gate)
    hidden = (pre_gate * sigmoid_gate * pre_up).astype(jnp.bfloat16)
    d_output = (-step_rates[:, None] * token_values.astype(jnp.float32)).astype(jnp.bfloat16)
    d_hidden = jnp.dot(d_output, down_b, preferred_element_type=jnp.float32)
    d_up = (d_hidden * pre_gate * sigmoid_gate).astype(jnp.bfloat16)
    d_gate = (d_hidden * pre_up * sigmoid_gate * (1.0 + pre_gate * (1.0 - sigmoid_gate))).astype(
        jnp.bfloat16
    )
    return (dot_cols(d_gate, token_keys), dot_cols(d_up, token_keys), dot_cols(d_output, hidden))


def renorm(weight, gradient):
    moved = weight - gradient
    keep = jnp.sqrt(jnp.sum(weight * weight, axis=1, keepdims=True))
    return moved * keep * lax.rsqrt(jnp.sum(moved * moved, axis=1, keepdims=True) + EPS_NORM)


def fast_apply(token_queries, gate_b, up_b, down_b):
    pre_gate = dot_rows(token_queries, gate_b)
    pre_up = dot_rows(token_queries, up_b)
    mixed = (pre_gate * jax.nn.sigmoid(pre_gate) * pre_up).astype(jnp.bfloat16)
    return dot_rows(mixed, down_b)


def normed_rows(fast_out, norm_gain):
    inverse = lax.rsqrt(jnp.mean(fast_out * fast_out, axis=1, keepdims=True) + EPS_NORM)
    return (fast_out * inverse * norm_gain[None, :]).astype(jnp.bfloat16)


def head_norm(projected, heads):
    count, features = projected.shape
    shaped = projected.reshape(count, heads, features // heads)
    shaped = shaped * lax.rsqrt(jnp.mean(shaped * shaped, axis=2, keepdims=True) + EPS_NORM)
    return shaped.reshape(count, features).astype(jnp.bfloat16)


def attend(q_rows, k_rows, v_rows, head_temper, half_span):
    heads = head_temper.shape[0]
    head_size = q_rows.shape[1] // heads
    query_count = q_rows.shape[0]
    key_count = k_rows.shape[0]
    offset = jnp.arange(key_count)[None, :] - half_span - jnp.arange(query_count)[:, None]
    inside = jnp.abs(offset) <= half_span

    def one_head(head):
        start = head * head_size
        query_h = lax.dynamic_slice_in_dim(q_rows, start, head_size, 1)
        key_h = lax.dynamic_slice_in_dim(k_rows, start, head_size, 1)
        value_h = lax.dynamic_slice_in_dim(v_rows, start, head_size, 1)
        scores = dot_rows(query_h, key_h) * (head_temper[head] / math.sqrt(head_size))
        scores = jnp.where(inside, scores, -1e30)
        highest = jnp.max(scores, axis=1, keepdims=True)
        weights = jnp.exp(scores - highest)
        weights = weights / jnp.sum(weights, axis=1, keepdims=True)
        return jnp.dot(weights.astype(jnp.bfloat16), value_h, preferred_element_type=jnp.float32)

    stacked = lax.map(one_head, jnp.arange(heads, dtype=jnp.int32))
    return jnp.transpose(stacked, (1, 0, 2)).reshape(query_count, heads * head_size)


def per_device(
    token_keys,
    token_values,
    token_queries,
    step_rates,
    fast_gate,
    fast_up,
    fast_down,
    norm_gain,
    proj_query,
    proj_key,
    proj_value,
    head_temper,
):
    gate_all, up_all, down_all = (
        lax.all_gather(fast_gate.astype(jnp.bfloat16), "col", axis=0, tiled=True),
        lax.all_gather(fast_up.astype(jnp.bfloat16), "col", axis=0, tiled=True),
        lax.all_gather(fast_down.astype(jnp.bfloat16), "col", axis=0, tiled=True),
    )
    grad_gate, grad_up, grad_down = fast_gradients(
        token_keys, token_values, step_rates, gate_all, up_all, down_all
    )
    block_gate, block_up, block_down = (
        lax.psum_scatter(grad_gate, "col", scatter_dimension=0, tiled=True),
        lax.psum_scatter(grad_up, "col", scatter_dimension=0, tiled=True),
        lax.psum_scatter(grad_down, "col", scatter_dimension=0, tiled=True),
    )
    owned_gate, owned_up, owned_down = lax.psum((block_gate, block_up, block_down), "row")
    new_gate = renorm(fast_gate, owned_gate)
    new_up = renorm(fast_up, owned_up)
    new_down = renorm(fast_down, owned_down)
    gate_new_all, up_new_all, down_new_all = (
        lax.all_gather(new_gate.astype(jnp.bfloat16), "col", axis=0, tiled=True),
        lax.all_gather(new_up.astype(jnp.bfloat16), "col", axis=0, tiled=True),
        lax.all_gather(new_down.astype(jnp.bfloat16), "col", axis=0, tiled=True),
    )
    fast_out = fast_apply(token_queries, gate_new_all, up_new_all, down_new_all)
    normed = normed_rows(fast_out, norm_gain)
    heads = head_temper.shape[0]
    query_n = head_norm(jnp.dot(normed, proj_query, preferred_element_type=jnp.float32), heads)
    key_n = head_norm(jnp.dot(normed, proj_key, preferred_element_type=jnp.float32), heads)
    value_b = jnp.dot(normed, proj_value, preferred_element_type=jnp.float32).astype(jnp.bfloat16)
    features = key_n.shape[1]
    half_span = token_keys.shape[0] // 2
    key_value = jnp.concatenate([key_n, value_b], axis=1)
    padded = padded_2(key_value, ((("row", "col"), 0),), half_span)
    attended = attend(query_n, padded[:, :features], padded[:, features:], head_temper, half_span)
    return (attended.astype(jnp.bfloat16), new_gate, new_up, new_down)


def solution(mesh):
    placed = (
        P(("row", "col"), None),
        P(("row", "col"), None),
        P(("row", "col"), None),
        P(("row", "col")),
        P("col", None),
        P("col", None),
        P("col", None),
        P(),
        P(),
        P(),
        P(),
        P(),
    )
    return jax.shard_map(
        per_device,
        mesh=mesh,
        in_specs=placed,
        out_specs=(P(("row", "col"), None), P("col", None), P("col", None), P("col", None)),
        check_vma=False,
    )
```

profile of v0, /device:TPU:1, one launch (start us, length us, event | category | flops | bytes accessed | tf_op | source)
XLA Modules:
  0.0 428.1 jit_solution(3889211581354217575)
XLA Ops:
  7.2 2.3 convert_element_type.64
  12.0 9.9 %all-gather.11.cloned.1.call-done = bf16[768,768]{1,0:T(8,128)(2,1)} async-done(((bf16[384,768]{1,0:T(8,128)(2,1)}), bf16[768,768]{1,0:T(8,128)(2,1)}) %all-gather.11.cloned.1.call-update) | async-done | bytes 1179664 | tf_op jit(solution)/shard_map/all_gather | solution.py:117
  21.9 3.6 fusion.32
  25.4 9.0 %all-gather.9.cloned.1.call-done = bf16[768,768]{1,0:T(8,128)(2,1)} async-done(((bf16[384,768]{1,0:T(8,128)(2,1)}), bf16[768,768]{1,0:T(8,128)(2,1)}) %all-gather.9.cloned.1.call-update) | async-done | bytes 1179664 | tf_op jit(solution)/shard_map/all_gather | solution.py:118
  34.4 3.2 fusion.31
  37.6 9.3 %all-gather.7.cloned.1.call-done = bf16[768,768]{1,0:T(8,128)(2,1)} async-done(((bf16[384,768]{1,0:T(8,128)(2,1)}), bf16[768,768]{1,0:T(8,128)(2,1)}) %all-gather.7.cloned.1.call-update) | async-done | bytes 1179664 | tf_op jit(solution)/shard_map/all_gather | solution.py:119
  47.0 2.5 fusion.19
  50.7 2.6 fusion.18
  53.4 4.2 fusion.16
  58.7 4.3 %fusion.17 = f32[768,768]{1,0:T(8,128)} fusion(f32[512,768]{1,0:T(8,128)} %fusion.31, f32[512,768]{1,0:T(8,128)} %fusion.32, bf16[512,768]{1,0:T(8,128)(2,1)S(1)} %copy-done.16, f32[512]{0:T(512)S(1)} %neg.10), kind=kOutput, calls=%fused_computation.47 | convolution fusion | flops 607518720 | bytes 6293504 | tf_op jit(solution)/shard_map/dot_general | solution.py:34
  64.5 13.3 %reduce-scatter.6.cloned.1.call-done = f32[384,768]{1,0:T(8,128)} async-done(((f32[768,768]{1,0:T(8,128)}), f32[384,768]{1,0:T(8,128)}) %reduce-scatter.6.cloned.1.call-update) | async-done | bytes 1179664 | tf_op jit(solution)/shard_map/reduce_scatter | solution.py:126
  77.8 13.2 %reduce-scatter.8.cloned.1.call-done = f32[384,768]{1,0:T(8,128)} async-done(((f32[768,768]{1,0:T(8,128)}), f32[384,768]{1,0:T(8,128)}) %reduce-scatter.8.cloned.1.call-update) | async-done | bytes 1179664 | tf_op jit(solution)/shard_map/reduce_scatter | solution.py:127
  91.1 163.5 %all-reduce.3.cloned.1.call-done = (f32[384,768]{1,0:T(8,128)}, f32[384,768]{1,0:T(8,128)}, f32[384,768]{1,0:T(8,128)}) async-done(((f32[384,768]{1,0:T(8,128)}, f32[384,768]{1,0:T(8,128)}, f32[384,768]{1,0:T(8,128)}), (f32[384,768]{1,0:T(8,128)}, f32[384,768]{1,0:T(8,128)}, f32[384,768]{1,0:T(8,128)})) %all-reduce.3.cloned.1.call-update) | async-done | bytes 3538960 | tf_op jit(solution)/shard_map/psum | solution.py:129
  259.5 2.9 fusion.24
  266.7 3.5 fusion.33
  270.2 8.5 %all-gather.15.cloned.1.call-done = bf16[768,768]{1,0:T(8,128)(2,1)} async-done(((bf16[384,768]{1,0:T(8,128)(2,1)}), bf16[768,768]{1,0:T(8,128)(2,1)}) %all-gather.15.cloned.1.call-update) | async-done | bytes 1179664 | tf_op jit(solution)/shard_map/all_gather | solution.py:135
  278.7 11.8 %all-gather.17.cloned.1.call-done = bf16[768,768]{1,0:T(8,128)(2,1)} async-done(((bf16[384,768]{1,0:T(8,128)(2,1)}), bf16[768,768]{1,0:T(8,128)(2,1)}) %all-gather.17.cloned.1.call-update) | async-done | bytes 1179664 | tf_op jit(solution)/shard_map/all_gather | solution.py:136
  290.5 4.0 multiply_reduce_fusion
  294.7 2.4 fusion.30
  306.1 2.4 fusion.29
  312.5 2.9 multiply_convert_fusion.1
  315.4 8.4 %collective-permute-done = bf16[256,1536]{1,0:T(8,128)(2,1)} collective-permute-done((bf16[256,1536]{1,0:T(8,128)(2,1)}, bf16[256,1536]{1,0:T(8,128)(2,1)}, u32[]{:S(2)}, u32[]{:S(2)}) %collective-permute-start) | collective-permute-done | bytes 786464 | tf_op jit(solution)/shard_map/ppermute | solution.py:18
  328.7 91.1 %while.11 = (s32[]{:T(128)}, bf16[12,512,64]{1,2,0:T(8,128)(2,1)S(1)}, s32[12]{0:T(128)S(1)}, bf16[512,768]{1,0:T(8,128)(2,1)}, bf16[1024,768]{1,0:T(8,128)(2,1)...) while((s32[]{:T(128)}, ...), condition=%wide.region_18.19_spmd.clone, body=%wide.region_15.18_spmd.clone.sunk | while | flops 139983872 | bytes 7094017 | solution.py:98
  333.1 1.9 fusion.57
  (161 shorter events, 84.8 us)
Async XLA Ops:
  7.2 287.6 %copy-start = (bf16[768,768]{1,0:T(8,128)(2,1)S(1)}, bf16[768,768]{1,0:T(8,128)(2,1)}, u32[]{:S(2)}) copy-start(bf16[768,768]{1,0:T(8,128)(2,1)} %param.23) | copy-start | bytes 3538948
  7.2 2.4 copy-start.3
  7.2 14.7 %all-gather.11.cloned.1.call-start = ((), (), s32[]{:S(2)}) async-start(), calls=%async_computation.5 | async-start | bytes 1769472 | tf_op jit(solution)/shard_map/all_gather | solution.py:117
  9.6 24.8 %all-gather.9.cloned.1.call-start = ((), (), s32[]{:S(2)}) async-start(), calls=%async_computation.4 | async-start | bytes 1769472 | tf_op jit(solution)/shard_map/all_gather | solution.py:118
  10.5 36.4 %all-gather.7.cloned.1.call-start = ((), (), s32[]{:S(2)}) async-start(), calls=%async_computation.3 | async-start | bytes 1769472 | tf_op jit(solution)/shard_map/all_gather | solution.py:119
  11.9 52.6 %reduce-scatter.4.cloned.1.call-start = ((), (), s32[]{:S(2)}) async-start(), calls=%async_computation.6 | async-start | bytes 3538944 | tf_op jit(solution)/shard_map/reduce_scatter | solution.py:125
  12.0 22.4 %copy-start.15 = (bf16[512,768]{1,0:T(8,128)(2,1)S(1)}, bf16[512,768]{1,0:T(8,128)(2,1)}, u32[]{:S(2)}) copy-start(bf16[512,768]{1,0:T(8,128)(2,1)} %param.14) | copy-start | bytes 2359300
  47.0 3.7 copy-start.19
  47.0 3.7 copy-start.20
  53.3 24.5 %reduce-scatter.6.cloned.1.call-start = ((), (), s32[]{:S(2)}) async-start(), calls=%async_computation.8 | async-start | bytes 3538944 | tf_op jit(solution)/shard_map/reduce_scatter | solution.py:126
  57.6 33.4 %reduce-scatter.8.cloned.1.call-start = ((), (), s32[]{:S(2)}) async-start(), calls=%async_computation.10 | async-start | bytes 3538944 | tf_op jit(solution)/shard_map/reduce_scatter | solution.py:127
  63.0 191.5 %all-reduce.3.cloned.1.call-start = ((), (), s32[]{:S(2)}) async-start(), calls=%async_computation.12 | async-start | bytes 7077888 | tf_op jit(solution)/shard_map/psum | solution.py:129
  91.0 163.6 %copy-start.2 = (f32[384,768]{1,0:T(8,128)S(1)}, f32[384,768]{1,0:T(8,128)}, u32[]{:S(2)}) copy-start(f32[384,768]{1,0:T(8,128)} %param.18) | copy-start | bytes 3538948
  91.0 175.7 %all-gather.13.cloned.1.call-start = ((), (), s32[]{:S(2)}) async-start(), calls=%async_computation.7 | async-start | bytes 1769472 | tf_op jit(solution)/shard_map/all_gather | solution.py:134
  254.6 1.7 copy-start.9
  257.9 20.8 %all-gather.15.cloned.1.call-start = ((), (), s32[]{:S(2)}) async-start(), calls=%async_computation.9 | async-start | bytes 1769472 | tf_op jit(solution)/shard_map/all_gather | solution.py:135
  259.5 3.2 copy-start.5
  262.4 2.1 copy-start.8
  262.5 28.1 %all-gather.17.cloned.1.call-start = ((), (), s32[]{:S(2)}) async-start(), calls=%async_computation.11 | async-start | bytes 1769472 | tf_op jit(solution)/shard_map/all_gather | solution.py:136
  270.2 24.3 %copy-start.12 = (f32[768]{0:T(1024)S(1)}, f32[768]{0:T(1024)}, u32[]{:S(2)}) copy-start(f32[768]{0:T(1024)} %param.21) | copy-start | bytes 9220
  301.1 1.9 copy-start.7
  303.2 2.9 copy-start.10
  304.5 19.3 %collective-permute-start = (bf16[256,1536]{1,0:T(8,128)(2,1)}, bf16[256,1536]{1,0:T(8,128)(2,1)}, u32[]{:S(2)}, u32[]{:S(2)}) collective-permute-start(bf16[256,1536]{1,0:T(8,128)(2,1)} %get-tuple-element.105), channel_id=1, source_target_pairs={{0,1},{1,2},{2,3},{3,4},{4,5},{5,6},{6,7},{7,8},{8,9},{9,10},{10,1... | collective-permute-start | bytes 2359304 | tf_op jit(solution)/shard_map/ppermute | solution.py:18
  306.1 19.3 %collective-permute-start.1 = (bf16[256,1536]{1,0:T(8,128)(2,1)}, bf16[256,1536]{1,0:T(8,128)(2,1)}, u32[]{:S(2)}, u32[]{:S(2)}) collective-permute-start(bf16[256,1536]{1,0:T(8,128)(2,1)} %get-tuple-element.106), channel_id=1, source_target_pairs={{1,0},{2,1},{3,2},{4,3},{5,4},{6,5},{7,6},{8,7},{9,8},{10,9},{11,1... | collective-permute-start | bytes 2359304 | tf_op jit(solution)/shard_map/ppermute | solution.py:20
  (9 other events, 12.5 us)
Sparse Core Ops, SparseCore 0:
  10.1 11.6 all-gather.10
  24.0 10.3 all-gather.8
  36.5 10.3 all-gather.6
  53.4 11.0 reduce-scatter.3
  66.7 11.0 reduce-scatter.5
  79.9 11.0 reduce-scatter.7
  98.3 156.2 all-reduce.2
  258.0 8.6 all-gather.12
  268.3 10.3 all-gather.14
  280.1 10.3 all-gather.16
where the time goes:
time: 429 us; the launch traced here: 428 us
  waiting for transfers between devices  251 us (59%)
  matrix products  65.3 us (15%)
  loops' own time  39.1 us (9%)
  other arithmetic  28.2 us (7%)
  local copies, waits for them, and re-layouts  28.1 us (7%)
  between operations  14.5 us (3%)
    psum x1, waiting for transfers between devices, per_device(): lax.psum((block_gate, block_up, block_down), 'row')  164 us
    another operation x1, loops' own time, attend(): stacked = lax.map(one_head, jnp.arange(heads, dtype=jnp.int32))  39.1 us
    dot_general x16, matrix products, dot_rows(): lax.dot_general(left, right, (((1,), (1,)), ((), ())), preferred_element_...  37.1 us
    reduce_scatter x1, waiting for transfers between devices, per_device(): lax.psum_scatter(grad_up, 'col', scatter_dimension=0, tiled=True)  13.3 us
    reduce_scatter x1, waiting for transfers between devices, per_device(): lax.psum_scatter(grad_down, 'col', scatter_dimension=0, tiled=True)  13.2 us
    all_gather x1, waiting for transfers between devices, per_device(): lax.all_gather(new_down.astype(jnp.bfloat16), 'col', axis=0, tiled=True)  11.8 us
    dot_general x3, matrix products, dot_cols(): lax.dot_general(left, right, (((0,), (0,)), ((), ())), preferred_element_...  11.2 us
    all_gather x1, waiting for transfers between devices, per_device(): lax.all_gather(fast_gate.astype(jnp.bfloat16), 'col', axis=0, tiled=True)  9.86 us
  transfers between devices with their start and end apart: 12, of which 12 were waited for; matrix products, arithmetic and copies ran while one was open for 9% of the time, Pallas kernels for 0%

commit v1 on v0

v1 whole, which is shorter than its diff:
```python
import functools
import math

import jax
import jax.numpy as jnp
from jax import lax
from jax.experimental import pallas as pl
from jax.experimental.pallas import tpu as pltpu
from jax.sharding import PartitionSpec as P

EPS_NORM = 1e-06
MESH = pl.DeviceIdType.MESH
VMEM = pltpu.VMEM
PART = 256
LIMIT = 50 * 1024 * 1024


def dot_rows(left, right):
    return lax.dot_general(
        left, right, (((1,), (1,)), ((), ())), preferred_element_type=jnp.float32
    )


def dot_cols(left, right):
    return lax.dot_general(
        left, right, (((0,), (0,)), ((), ())), preferred_element_type=jnp.float32
    )


def exchange_kernel(n_row, n_col, gate, up, down, queries, weights, halo, w_send, w_recv, h_send, h_recv):
    row, col = lax.axis_index("row"), lax.axis_index("col")
    total = n_row * n_col
    place = row * n_col + col
    after, before = lax.rem(place + 1, total), lax.rem(place + total - 1, total)
    after_id = (after // n_col, lax.rem(after, n_col))
    before_id = (before // n_col, lax.rem(before, n_col))
    peers = [(row, lax.rem(col + step, n_col)) for step in range(1, n_col)]
    barrier = pltpu.get_barrier_semaphore()
    for target in peers + [after_id, before_id]:
        pl.semaphore_signal(barrier, inc=1, device_id=target, device_id_type=MESH)
    for m, source in enumerate((gate, up, down)):
        weights[m, col] = source[...].astype(jnp.bfloat16)
    pl.semaphore_wait(barrier, n_col + 1)
    copies = []
    for m in range(3):
        for step, peer in enumerate(peers):
            copies.append(
                pltpu.make_async_remote_copy(
                    src_ref=weights.at[m, col],
                    dst_ref=weights.at[m, col],
                    send_sem=w_send.at[m, step],
                    recv_sem=w_recv.at[m, step],
                    device_id=peer,
                    device_id_type=MESH,
                )
            )
    half = halo.shape[1]
    count = queries.shape[0]
    copies.append(
        pltpu.make_async_remote_copy(
            src_ref=queries.at[pl.ds(count - half, half)],
            dst_ref=halo.at[0],
            send_sem=h_send.at[0],
            recv_sem=h_recv.at[0],
            device_id=after_id,
            device_id_type=MESH,
        )
    )
    copies.append(
        pltpu.make_async_remote_copy(
            src_ref=queries.at[pl.ds(0, half)],
            dst_ref=halo.at[1],
            send_sem=h_send.at[1],
            recv_sem=h_recv.at[1],
            device_id=before_id,
            device_id_type=MESH,
        )
    )
    for copy in copies:
        copy.start()
    for copy in copies:
        copy.wait()


def exchange(n_row, n_col, gate, up, down, queries):
    rows, features = gate.shape
    half = queries.shape[0] // 2
    return pl.pallas_call(
        functools.partial(exchange_kernel, n_row, n_col),
        out_shape=(
            jax.ShapeDtypeStruct((3, n_col, rows, features), jnp.bfloat16),
            jax.ShapeDtypeStruct((2, half, features), jnp.bfloat16),
        ),
        in_specs=[pl.BlockSpec(memory_space=VMEM)] * 3 + [pl.BlockSpec(memory_space=pl.ANY)],
        out_specs=(pl.BlockSpec(memory_space=VMEM), pl.BlockSpec(memory_space=pl.ANY)),
        scratch_shapes=[
            pltpu.SemaphoreType.DMA((3, max(n_col - 1, 1))),
            pltpu.SemaphoreType.DMA((3, max(n_col - 1, 1))),
            pltpu.SemaphoreType.DMA((2,)),
            pltpu.SemaphoreType.DMA((2,)),
        ],
        compiler_params=pltpu.CompilerParams(
            collective_id=0, has_side_effects=True, vmem_limit_bytes=LIMIT
        ),
        name="exchange",
    )(gate, up, down, queries)


def gradient_kernel(n_col, keys, values, rates, weights, out, hidden, d_output, d_up, d_gate):
    chunk = keys.shape[0] // 2
    rows = weights.shape[1] // n_col
    parts = keys.shape[1] // PART
    for start in range(0, keys.shape[0], chunk):
        span = pl.ds(start, chunk)
        token = keys[span, :]
        pre_gate = dot_rows(token, weights[0])
        pre_up = dot_rows(token, weights[1])
        d_out = (-rates[span, :] * values[span, :].astype(jnp.float32)).astype(jnp.bfloat16)
        d_output[span, :] = d_out
        d_hidden = jnp.dot(d_out, weights[2], preferred_element_type=jnp.float32)
        sig = jax.nn.sigmoid(pre_gate)
        silu = pre_gate * sig
        hidden[span, :] = (silu * pre_up).astype(jnp.bfloat16)
        d_up[span, :] = (d_hidden * silu).astype(jnp.bfloat16)
        d_gate[span, :] = (d_hidden * pre_up * sig * (1.0 + pre_gate * (1.0 - sig))).astype(jnp.bfloat16)
    for m, (left, right) in enumerate(((d_gate, keys), (d_up, keys), (d_output, hidden))):
        turned = left[...]
        for p in range(parts):
            summed = dot_cols(turned, right[:, p * PART : (p + 1) * PART]).astype(jnp.bfloat16)
            for c in range(n_col):
                out[p, c, m * rows : (m + 1) * rows, :] = summed[c * rows : (c + 1) * rows, :]


def gradients(n_col, keys, values, rates, weights):
    tokens, features = keys.shape
    rows = weights.shape[1] // n_col
    parts = features // PART
    return pl.pallas_call(
        functools.partial(gradient_kernel, n_col),
        out_shape=jax.ShapeDtypeStruct((parts, n_col, 3 * rows, PART), jnp.bfloat16),
        in_specs=[pl.BlockSpec(memory_space=VMEM)] * 4,
        out_specs=pl.BlockSpec(memory_space=VMEM),
        scratch_shapes=[VMEM((tokens, features), jnp.bfloat16)] * 4,
        compiler_params=pltpu.CompilerParams(vmem_limit_bytes=LIMIT),
        cost_estimate=pl.CostEstimate(
            flops=12 * tokens * features * features, bytes_accessed=9 * 2**20, transcendentals=0
        ),
        name="gradients",
    )(keys, values, rates, weights)


def update_kernel(
    n_row, n_col, bits, grads, gate, up, down, out,
    held, from_col, *rest,
):
    landing, (total, fast, c_send, c_recv, r_send, r_recv, g_send, g_recv, o_send, o_recv, f_sem) = (
        rest[:bits], rest[bits:]
    )
    row, col = lax.axis_index("row"), lax.axis_index("col")
    parts = grads.shape[0]
    unit = grads.shape[-2]
    mine = [lax.rem(row // (1 << b), 2) for b in range(bits)]
    peers = [(row, lax.rem(col + step, n_col)) for step in range(1, n_col)]
    partners = [(row + (1 - 2 * mine[b]) * (1 << b), col) for b in range(bits)]

    barrier = pltpu.get_barrier_semaphore()
    for target in peers + partners:
        pl.semaphore_signal(barrier, inc=1, device_id=target, device_id_type=MESH)
    rows = gate.shape[0]
    fills = [
        pltpu.make_async_copy(source, fast.at[pl.ds(m * rows, rows)], f_sem.at[m])
        for m, source in enumerate((gate, up, down))
    ]
    for fill in fills:
        fill.start()
    pl.semaphore_wait(barrier, len(peers) + len(partners))

    def planes(fixed):
        return tuple(fixed.get(b, slice(None)) for b in reversed(range(bits)))

    free = min(3, bits)

    def order(p):
        return [(p + s) % free for s in range(free)] + list(range(free, bits))

    first = {}
    for p in range(parts):
        for step, peer in enumerate(peers):
            first[p, step] = pltpu.make_async_remote_copy(
                src_ref=grads.at[p, peer[1]],
                dst_ref=from_col.at[step, p],
                send_sem=c_send.at[p, step],
                recv_sem=c_recv.at[p, step],
                device_id=peer,
                device_id_type=MESH,
            )
            first[p, step].start()

    halvings = {}

    def halve(p, s):
        b = order(p)[s]
        fixed = {order(p)[t]: mine[order(p)[t]] for t in range(s)}
        fixed[b] = 1 - mine[b]
        halvings[p, s] = pltpu.make_async_remote_copy(
            src_ref=held.at[(p,) + planes(fixed)],
            dst_ref=landing[s].at[p],
            send_sem=r_send.at[p, s],
            recv_sem=r_recv.at[p, s],
            device_id=partners[b],
            device_id_type=MESH,
        )
        halvings[p, s].start()

    for p in range(parts):
        for step in range(len(peers)):
            first[p, step].wait_recv()
        summed = grads[p, col].astype(jnp.float32)
        for step in range(len(peers)):
            summed = summed + from_col[step, p].astype(jnp.float32)
        held[p] = summed.astype(jnp.bfloat16)
        halve(p, 0)
    for s in range(bits):
        for p in range(parts):
            halvings[p, s].wait_recv()
            fixed = {order(p)[t]: mine[order(p)[t]] for t in range(s + 1)}
            index = (p,) + planes(fixed)
            summed = held[index].astype(jnp.float32) + landing[s][p].astype(jnp.float32)
            if s < bits - 1:
                held[index] = summed.astype(jnp.bfloat16)
                halve(p, s + 1)
            else:
                total[:, p * PART : (p + 1) * PART] = summed

    for fill in fills:
        fill.wait()
    if unit % 8 == 0:
        old = fast[pl.ds(pl.multiple_of(row * unit, 8), unit), :]
    else:
        old = sum(
            jnp.where(row == r, fast[r * unit : (r + 1) * unit, :], 0.0) for r in range(n_row)
        )
    moved = old - total[...]
    keep = jnp.sqrt(jnp.sum(old * old, axis=1, keepdims=True))
    new = moved * keep * lax.rsqrt(jnp.sum(moved * moved, axis=1, keepdims=True) + EPS_NORM)
    own = planes({b: mine[b] for b in range(bits)})
    doublings, handed = {}, {}

    def double(p, s):
        b = order(p)[s]
        part = (p, col) + planes({order(p)[t]: mine[order(p)[t]] for t in range(s + 1)})
        doublings[p, s] = pltpu.make_async_remote_copy(
            src_ref=out.at[part],
            dst_ref=out.at[part],
            send_sem=g_send.at[p, s],
            recv_sem=g_recv.at[p, s],
            device_id=partners[b],
            device_id_type=MESH,
        )
        doublings[p, s].start()

    for p in range(parts):
        out[(p, col) + own] = new[:, p * PART : (p + 1) * PART].astype(jnp.bfloat16)
        double(p, bits - 1)
    for s in reversed(range(bits)):
        for p in range(parts):
            doublings[p, s].wait_recv()
            if s > 0:
                double(p, s - 1)
            else:
                for step, peer in enumerate(peers):
                    handed[p, step] = pltpu.make_async_remote_copy(
                        src_ref=out.at[p, col],
                        dst_ref=out.at[p, col],
                        send_sem=o_send.at[p, step],
                        recv_sem=o_recv.at[p, step],
                        device_id=peer,
                        device_id_type=MESH,
                    )
                    handed[p, step].start()
    for copy in handed.values():
        copy.wait_recv()
    for group in (first, halvings, doublings, handed):
        for copy in group.values():
            copy.wait_send()


def update(n_row, n_col, grads, gate, up, down):
    parts, _, stacked, width = grads.shape
    bits = n_row.bit_length() - 1
    unit = stacked // n_row
    block = (2,) * bits + (unit, width)
    grads = grads.reshape((parts, n_col) + block)
    features = gate.shape[1]
    step = max(n_col - 1, 1)
    dma = pltpu.SemaphoreType.DMA
    landing = [VMEM((parts,) + (2,) * (bits - 1 - s) + (unit, width), jnp.bfloat16) for s in range(bits)]
    new = pl.pallas_call(
        functools.partial(update_kernel, n_row, n_col, bits),
        out_shape=jax.ShapeDtypeStruct(grads.shape, jnp.bfloat16),
        in_specs=[pl.BlockSpec(memory_space=VMEM)] + [pl.BlockSpec(memory_space=pl.ANY)] * 3,
        out_specs=pl.BlockSpec(memory_space=VMEM),
        scratch_shapes=[
            VMEM((parts,) + block, jnp.bfloat16),
            VMEM((step, parts) + block, jnp.bfloat16),
            *landing,
            VMEM((unit, features), jnp.float32),
            VMEM((stacked, features), jnp.float32),
            dma((parts, step)),
            dma((parts, step)),
            dma((parts, bits)),
            dma((parts, bits)),
            dma((parts, bits)),
            dma((parts, bits)),
            dma((parts, step)),
            dma((parts, step)),
            dma((3,)),
        ],
        compiler_params=pltpu.CompilerParams(
            collective_id=1, has_side_effects=True, vmem_limit_bytes=LIMIT
        ),
        name="update",
    )(grads, gate, up, down)
    return new.reshape(parts, n_col, stacked, width)


def attend_kernel(
    n_col, heads, temper, queries, halo, weights, gain, proj_q, proj_k, proj_v,
    attended, new_gate, new_up, new_down, query_n, key_n, value_b, bias,
):
    parts = weights.shape[0]
    rows = weights.shape[2] // 3
    tokens, features = queries.shape
    half = tokens // 2
    size = features // heads
    col = lax.axis_index("col")
    for m, target in enumerate((new_gate, new_up, new_down)):
        for p in range(parts):
            target[:, p * PART : (p + 1) * PART] = weights[p, col, m * rows : (m + 1) * rows, :].astype(jnp.float32)

    def whole(m, p):
        return jnp.concatenate(
            [weights[p, c, m * rows : (m + 1) * rows, :] for c in range(n_col)], axis=0
        )

    def apply(m, left):
        return sum(dot_rows(left[:, p * PART : (p + 1) * PART], whole(m, p)) for p in range(parts))

    group_r = lax.broadcasted_iota(jnp.int32, (PART, PART), 0) // size
    group_c = lax.broadcasted_iota(jnp.int32, (PART, PART), 1) // size
    same = jnp.where(group_r == group_c, 1.0 / size, 0.0).astype(jnp.bfloat16)

    def head_norm(projected):
        pieces = []
        for p in range(parts):
            piece = projected[:, p * PART : (p + 1) * PART]
            square = piece * piece
            top = square.astype(jnp.bfloat16)
            rest = (square - top.astype(jnp.float32)).astype(jnp.bfloat16)
            mean = jnp.dot(top, same, preferred_element_type=jnp.float32) + jnp.dot(
                rest, same, preferred_element_type=jnp.float32
            )
            pieces.append((piece * lax.rsqrt(mean + EPS_NORM)).astype(jnp.bfloat16))
        return jnp.concatenate(pieces, axis=1)

    def project(normed, proj):
        return jnp.dot(normed, proj[...], preferred_element_type=jnp.float32)

    for own in (True, False):
        tokens_in = queries[...] if own else jnp.concatenate([halo[0], halo[1]], axis=0)
        pre_gate = apply(0, tokens_in)
        pre_up = apply(1, tokens_in)
        mixed = (pre_gate * jax.nn.sigmoid(pre_gate) * pre_up).astype(jnp.bfloat16)
        fast_out = apply(2, mixed)
        inverse = lax.rsqrt(jnp.mean(fast_out * fast_out, axis=1, keepdims=True) + EPS_NORM)
        normed = (fast_out * inverse * gain[...]).astype(jnp.bfloat16)
        keys = head_norm(project(normed, proj_k))
        values = project(normed, proj_v).astype(jnp.bfloat16)
        if own:
            query_n[...] = head_norm(project(normed, proj_q))
            key_n[half : half + tokens, :] = keys
            value_b[half : half + tokens, :] = values
        else:
            key_n[0:half, :] = keys[:half]
            value_b[0:half, :] = values[:half]
            key_n[half + tokens :, :] = keys[half:]
            value_b[half + tokens :, :] = values[half:]

    at = lax.broadcasted_iota(jnp.int32, (half, 3 * half), 1) - lax.broadcasted_iota(
        jnp.int32, (half, 3 * half), 0
    )
    bias[...] = jnp.where((at >= 0) & (at <= 2 * half), 0.0, -1e30)
    pair = 128 // size
    lane = lax.broadcasted_iota(jnp.int32, (half, 128), 1) // size
    ones = jnp.ones((3 * half, 128), jnp.bfloat16)

    def one_pair(j, carry):
        lanes = pl.ds(pl.multiple_of(j * 128, 128), 128)
        for block in range(2):
            span = pl.ds(block * half, half)
            window = pl.ds(block * half, 3 * half)
            query = query_n[span, lanes]
            key = key_n[window, lanes]
            value = jnp.concatenate([value_b[window, lanes], ones], axis=1)
            result = jnp.zeros((half, 128), jnp.float32)
            for h in range(pair):
                scale = temper[j * pair + h] * (math.log2(math.e) / math.sqrt(size))
                scores = dot_rows(jnp.where(lane == h, query, jnp.zeros_like(query)), key) + bias[...]
                highest = jnp.max(scores, axis=1, keepdims=True)
                weight = jnp.exp2((scores - highest) * scale).astype(jnp.bfloat16)
                both = jnp.dot(weight, value, preferred_element_type=jnp.float32)
                result = jnp.where(lane == h, both[:, :128] / both[:, 128:], result)
            attended[span, lanes] = result.astype(jnp.bfloat16)
        return carry

    lax.fori_loop(0, features // 128, one_pair, 0)


def attend(n_col, queries, halo, weights, gain, proj_q, proj_k, proj_v, temper):
    tokens, features = queries.shape
    rows = weights.shape[2] // 3
    half = tokens // 2
    vmem = pl.BlockSpec(memory_space=VMEM)
    square = jax.ShapeDtypeStruct((rows, features), jnp.float32)
    return pl.pallas_call(
        functools.partial(attend_kernel, n_col, temper.shape[0]),
        out_shape=(jax.ShapeDtypeStruct((tokens, features), jnp.bfloat16), square, square, square),
        in_specs=[pl.BlockSpec(memory_space=pltpu.SMEM)] + [vmem] * 7,
        out_specs=(vmem,) * 4,
        scratch_shapes=[
            VMEM((tokens, features), jnp.bfloat16),
            VMEM((2 * tokens, features), jnp.bfloat16),
            VMEM((2 * tokens, features), jnp.bfloat16),
            VMEM((half, 3 * half), jnp.float32),
        ],
        compiler_params=pltpu.CompilerParams(vmem_limit_bytes=LIMIT),
        name="attend",
    )(temper, queries, halo, weights, gain[None, :], proj_q, proj_k, proj_v)


def per_device(
    n_row,
    n_col,
    token_keys,
    token_values,
    token_queries,
    step_rates,
    fast_gate,
    fast_up,
    fast_down,
    norm_gain,
    proj_query,
    proj_key,
    proj_value,
    head_temper,
):
    weights, halo = exchange(n_row, n_col, fast_gate, fast_up, fast_down, token_queries)
    weights = weights.reshape(3, -1, fast_gate.shape[1])
    grads = gradients(n_col, token_keys, token_values, step_rates[:, None], weights)
    new = update(n_row, n_col, grads, fast_gate, fast_up, fast_down)
    return attend(
        n_col, token_queries, halo, new, norm_gain, proj_query, proj_key, proj_value, head_temper
    )


def solution(mesh):
    placed = (
        P(("row", "col"), None),
        P(("row", "col"), None),
        P(("row", "col"), None),
        P(("row", "col")),
        P("col", None),
        P("col", None),
        P("col", None),
        P(),
        P(),
        P(),
        P(),
        P(),
    )
    return jax.shard_map(
        functools.partial(per_device, mesh.shape["row"], mesh.shape["col"]),
        mesh=mesh,
        in_specs=placed,
        out_specs=(P(("row", "col"), None), P("col", None), P("col", None), P("col", None)),
        check_vma=False,
    )
```

time: 429 us -> 108 us (0.25)
  waiting for transfers between devices: 251 us -> 0 us
  Pallas kernels: 0 us -> 102 us
  matrix products: 65.3 us -> 0 us
  loops' own time: 39.1 us -> 0 us
  other arithmetic: 28.2 us -> 0 us
  local copies, waits for them, and re-layouts: 28.1 us -> 5.23 us
  between operations: 14.5 us -> 0.77 us
    psum x1 -> x0, waiting for transfers between devices: 164 us -> none  [per_device(): lax.psum((block_gate, block_up, block_down), 'row')]
    pallas_call x0 -> x4, Pallas kernels: none -> 102 us  [the longest x1 55.3 us: update(): pl.pallas_call(functools.partial(update_kernel, n_row, n_col, bits), out_...]
    dot_general x35 -> x0, matrix products: 65.3 us -> none  [the longest x16 37.1 us: dot_rows(): lax.dot_general(left, right, (((1,), (1,)), ((), ())), preferred_element_...]
    all_gather x6 -> x0, waiting for transfers between devices: 49.1 us -> none  [the longest x1 11.8 us: per_device(): lax.all_gather(new_down.astype(jnp.bfloat16), 'col', axis=0, tiled=True)]
    another operation x1 -> x0, loops' own time: 39.1 us -> none  [attend(): stacked = lax.map(one_head, jnp.arange(heads, dtype=jnp.int32))]
    reduce_scatter x3 -> x0, waiting for transfers between devices: 27.9 us -> none  [the longest x1 13.3 us: per_device(): lax.psum_scatter(grad_up, 'col', scatter_dimension=0, tiled=True)]
    dynamic_slice x24 -> x0, local copies, waits for them, and re-layouts: 14.1 us -> none  [the longest x12 7.04 us: one_head(): head_temper[head] / math.sqrt(head_size)]
    convert_element_type x9 -> x0, other arithmetic: 13.4 us -> none  [the longest x2 3.12 us: head_norm(): return shaped.reshape(count, features).astype(jnp.bfloat16)]
  transfers between devices with their start and end apart: 12 -> 0, of which waited for: 12 -> 0; matrix products, arithmetic and copies ran while one was open for 9% -> 0% of each run, Pallas kernels for 0% -> 0%
where the time goes in v1:
time: 108 us
  Pallas kernels  102 us (94%)
  local copies, waits for them, and re-layouts  5.23 us (5%)
    pallas_call x1, Pallas kernels, update(): pl.pallas_call(functools.partial(update_kernel, n_row, n_col, bits), out_...  55.3 us
    pallas_call x1, Pallas kernels, attend(): pl.pallas_call(functools.partial(attend_kernel, n_col, temper.shape[0]),...  22.8 us
    pallas_call x1, Pallas kernels, exchange(): pl.pallas_call(functools.partial(exchange_kernel, n_row, n_col), out_shap...  15.3 us
    pallas_call x1, Pallas kernels, gradients(): pl.pallas_call(functools.partial(gradient_kernel, n_col), out_shape=jax.S...  8.22 us
    unnamed x24, local copies, waits for them, and re-layouts  3.72 us

profile of v1, /device:TPU:1, one launch (start us, length us, event | category | flops | bytes accessed | tf_op | source)
XLA Modules:
  0.0 107.7 jit_solution(10617793904297870720)
XLA Ops:
  0.6 0.7 broadcast_in_dim.7.gain
  1.3 0.8 copy.16.rates
  2.1 0.0 copy-start
  2.2 1.3 %copy-done = f32[384,768]{1,0:T(8,128)S(1)} copy-done((f32[384,768]{1,0:T(8,128)S(1)}, f32[384,768]{1,0:T(8,128)}, u32[]{:S(2)}) %copy-start) | copy-done | bytes 1179672
  3.4 1.3 %copy-done.2 = f32[384,768]{1,0:T(8,128)S(1)} copy-done((f32[384,768]{1,0:T(8,128)S(1)}, f32[384,768]{1,0:T(8,128)}, u32[]{:S(2)}) %copy-start.2) | copy-done | bytes 1179672
  4.7 1.1 %copy-done.5 = bf16[512,768]{1,0:T(8,128)(2,1)S(1)} copy-done((bf16[512,768]{1,0:T(8,128)(2,1)S(1)}, bf16[512,768]{1,0:T(8,128)(2,1)}, u32[]{:S(2)}) %copy-start.5) | copy-done | bytes 786456
  5.8 15.3 %exchange.1 = (bf16[3,2,384,768]{3,2,1,0:T(8,128)(2,1)}, bf16[2,256,768]{2,1,0:T(8,128)(2,1)S(1)}) custom-call(f32[384,768]{1,0:T(8,128)S(1)} %copy-done, f32[384,768]{1,0:T(8,128)S(1)} %copy-done.2, f32[384,768]{1,0:T(8,128)} %down.3, bf16[512,768]{1,0:T(8,128)(2,1)S(1)} %copy-done.5), custom_call_target="tpu_custom_call" | custom-call | tf_op jit(solution)/shard_map/exchange/pallas_call | solution.py:88
  21.2 0.0 copy-done.10
  21.2 0.0 copy-done.11
  21.2 0.0 copy-start.1
  21.2 0.0 copy-start.3
  21.2 0.0 copy-start.4
  21.2 8.2 %gradients.1 = bf16[3,2,1152,256]{3,2,1,0:T(8,128)(2,1)} custom-call(bf16[512,768]{1,0:T(8,128)(2,1)S(1)} %copy-done.10, bf16[512,768]{1,0:T(8,128)(2,1)S(1)} %copy-done.11, f32[512,1]{1,0:T(8,128)S(1)} %copy.16.rates, bf16[3,768,768]{2,1,0:T(8,128)(2,1)} %bitcast.7), custom_call_target="tpu_custom_call" | custom-call | flops 3623878656 | bytes 9437184 | tf_op jit(solution)/shard_map/gradients/pallas_call | solution.py:138
  29.4 0.0 copy-done.1
  29.4 0.0 copy-start.6
  29.5 0.0 copy-start.7
  29.5 0.0 copy-start.8
  29.5 0.0 copy-start.9
  29.5 55.3 %update.1 = bf16[3,2,2,2,2,2,72,256]{7,6,5,4,3,2,1,0:T(8,128)(2,1)} custom-call(bf16[3,2,2,2,2,2,72,256]{7,6,5,4,3,2,1,0:T(8,128)(2,1)} %bitcast.5, f32[384,768]{1,0:T(8,128)S(1)} %copy-done.1, f32[384,768]{1,0:T(8,128)S(1)} %copy-done.3, f32[384,768]{1,0:T(8,128)S(1)} %copy-done.4), custom_call_target="tpu_custom_call" | custom-call | tf_op jit(solution)/shard_map/update/pallas_call | solution.py:298
  84.8 0.0 copy-done.6
  84.9 0.0 copy-done.7
  84.9 0.0 copy-done.8
  84.9 0.0 copy-done.9
  84.9 22.8 %attend.1 = (bf16[512,768]{1,0:T(8,128)(2,1)}, f32[384,768]{1,0:T(8,128)}, f32[384,768]{1,0:T(8,128)}, f32[384,768]{1,0:T(8,128)}) custom-call(f32[12]{0:T(128)S(1)} %copy-done.9, bf16[512,768]{1,0:T(8,128)(2,1)S(1)} %copy-done.6, bf16[2,256,768]{2,1,0:T(8,128)(2,1)S(1)} %get-tuple-element.6.halo, bf16[3,2,1152,256]{3,2,1,0:T(8,128)(2,1)} %bitcast.4, ...), custom_call_target="tpu_custom_call" | custom-call | tf_op jit(solution)/shard_map/attend/pallas_call | solution.py:425
  (6 shorter events, 0.0 us)
Async XLA Ops:
  2.1 1.3 %copy-start = (f32[384,768]{1,0:T(8,128)S(1)}, f32[384,768]{1,0:T(8,128)}, u32[]{:S(2)}) copy-start(f32[384,768]{1,0:T(8,128)} %gate.3) | copy-start | bytes 3538948
  3.4 1.3 %copy-start.2 = (f32[384,768]{1,0:T(8,128)S(1)}, f32[384,768]{1,0:T(8,128)}, u32[]{:S(2)}) copy-start(f32[384,768]{1,0:T(8,128)} %up.3) | copy-start | bytes 3538948
  4.7 1.1 %copy-start.5 = (bf16[512,768]{1,0:T(8,128)(2,1)S(1)}, bf16[512,768]{1,0:T(8,128)(2,1)}, u32[]{:S(2)}) copy-start(bf16[512,768]{1,0:T(8,128)(2,1)} %queries.3) | copy-start | bytes 2359300
  5.8 15.3 %copy-start.10 = (bf16[512,768]{1,0:T(8,128)(2,1)S(1)}, bf16[512,768]{1,0:T(8,128)(2,1)}, u32[]{:S(2)}) copy-start(bf16[512,768]{1,0:T(8,128)(2,1)} %keys.1) | copy-start | bytes 2359300
  5.8 15.3 %copy-start.11 = (bf16[512,768]{1,0:T(8,128)(2,1)S(1)}, bf16[512,768]{1,0:T(8,128)(2,1)}, u32[]{:S(2)}) copy-start(bf16[512,768]{1,0:T(8,128)(2,1)} %values.1) | copy-start | bytes 2359300
  21.2 8.3 %copy-start.1 = (f32[384,768]{1,0:T(8,128)S(1)}, f32[384,768]{1,0:T(8,128)}, u32[]{:S(2)}) copy-start(f32[384,768]{1,0:T(8,128)} %gate.3) | copy-start | bytes 3538948
  21.2 8.3 %copy-start.3 = (f32[384,768]{1,0:T(8,128)S(1)}, f32[384,768]{1,0:T(8,128)}, u32[]{:S(2)}) copy-start(f32[384,768]{1,0:T(8,128)} %up.3) | copy-start | bytes 3538948
  21.2 8.2 %copy-start.4 = (f32[384,768]{1,0:T(8,128)S(1)}, f32[384,768]{1,0:T(8,128)}, u32[]{:S(2)}) copy-start(f32[384,768]{1,0:T(8,128)} %down.3) | copy-start | bytes 3538948
  29.4 55.4 %copy-start.6 = (bf16[512,768]{1,0:T(8,128)(2,1)S(1)}, bf16[512,768]{1,0:T(8,128)(2,1)}, u32[]{:S(2)}) copy-start(bf16[512,768]{1,0:T(8,128)(2,1)} %queries.3) | copy-start | bytes 2359300
  29.5 55.4 %copy-start.7 = (bf16[768,768]{1,0:T(8,128)(2,1)S(1)}, bf16[768,768]{1,0:T(8,128)(2,1)}, u32[]{:S(2)}) copy-start(bf16[768,768]{1,0:T(8,128)(2,1)} %proj_q.1) | copy-start | bytes 3538948
  29.5 55.4 %copy-start.8 = (bf16[768,768]{1,0:T(8,128)(2,1)S(1)}, bf16[768,768]{1,0:T(8,128)(2,1)}, u32[]{:S(2)}) copy-start(bf16[768,768]{1,0:T(8,128)(2,1)} %proj_k.1) | copy-start | bytes 3538948
  29.5 55.4 %copy-start.9 = (f32[12]{0:T(128)S(1)}, f32[12]{0:T(128)}, u32[]{:S(2)}) copy-start(f32[12]{0:T(128)} %temper.1) | copy-start | bytes 148

commit v2 on v1

v2 whole, which is shorter than its diff:
```python
import functools
import math

import jax
import jax.numpy as jnp
from jax import lax
from jax.experimental import pallas as pl
from jax.experimental.pallas import tpu as pltpu
from jax.sharding import PartitionSpec as P

EPS_NORM = 1e-06
MESH = pl.DeviceIdType.MESH
VMEM = pltpu.VMEM
PART = 256
WIDTH = 128
LIMIT = 60 * 1024 * 1024


def dot_rows(left, right):
    return lax.dot_general(
        left, right, (((1,), (1,)), ((), ())), preferred_element_type=jnp.float32
    )


def update_kernel(
    n_row, n_col, bits,
    gate, up, down, keys_in, values_in, queries, rates,
    out_far, halo,
    out, fast, weights, keys, values, left, hidden, grads, held, from_col, *rest,
):
    landing, (
        total, f_sem, t_sem, x_sem, w_send, w_recv, h_send, h_recv,
        c_send, c_recv, r_send, r_recv, g_send, g_recv, o_send, o_recv,
    ) = rest[:bits], rest[bits:]
    row, col = lax.axis_index("row"), lax.axis_index("col")
    parts = grads.shape[0]
    unit = total.shape[0]
    rows = gate.shape[0]
    count = keys.shape[0]
    half = count // 2
    devices = n_row * n_col
    place = row * n_col + col
    after, before = lax.rem(place + 1, devices), lax.rem(place + devices - 1, devices)
    after_id = (after // n_col, lax.rem(after, n_col))
    before_id = (before // n_col, lax.rem(before, n_col))
    mine = [lax.rem(row // (1 << b), 2) for b in range(bits)]
    peers = [(row, lax.rem(col + step, n_col)) for step in range(1, n_col)]
    partners = [(row + (1 - 2 * mine[b]) * (1 << b), col) for b in range(bits)]

    barrier = pltpu.get_barrier_semaphore()
    everyone = peers + [after_id, before_id] + partners
    for target in everyone:
        pl.semaphore_signal(barrier, inc=1, device_id=target, device_id_type=MESH)
    fills = [
        pltpu.make_async_copy(source, fast.at[pl.ds(m * rows, rows)], f_sem.at[m])
        for m, source in enumerate((gate, up, down))
    ]
    tokens = [
        pltpu.make_async_copy(keys_in, keys, t_sem.at[0]),
        pltpu.make_async_copy(values_in, values, t_sem.at[1]),
    ]
    for copy in (fills[0], tokens[0], fills[1], fills[2], tokens[1]):
        copy.start()

    def remote(source, target, send, recv, device):
        copy = pltpu.make_async_remote_copy(
            src_ref=source, dst_ref=target, send_sem=send, recv_sem=recv,
            device_id=device, device_id_type=MESH,
        )
        copy.start()
        return copy

    given = {}
    for m in range(3):
        fills[m].wait()
        weights[m, col] = fast[m * rows : (m + 1) * rows, :].astype(jnp.bfloat16)
        if m == 0:
            pl.semaphore_wait(barrier, len(everyone))
        for step, peer in enumerate(peers):
            given[m, step] = remote(
                weights.at[m, col], weights.at[m, col], w_send.at[m, step], w_recv.at[m, step], peer
            )
    edges = {
        0: remote(queries.at[pl.ds(count - half, half)], halo.at[0], h_send.at[0], h_recv.at[0], after_id),
        1: remote(queries.at[pl.ds(0, half)], halo.at[1], h_send.at[1], h_recv.at[1], before_id),
    }

    def ready(m):
        for step in range(len(peers)):
            given[m, step].wait_recv()
        return weights[m].reshape(n_col * rows, weights.shape[3])

    for token in tokens:
        token.wait()
    token = keys[...]
    size = min(128, count)
    same = lax.broadcasted_iota(jnp.int32, (size, size), 0) == lax.broadcasted_iota(
        jnp.int32, (size, size), 1
    )
    rate_column = jnp.concatenate(
        [
            jnp.sum(
                jnp.where(same, rates[start : start + size][None, :], 0.0), axis=1, keepdims=True
            )
            for start in range(0, count, size)
        ],
        axis=0,
    )
    d_out = (-rate_column * values[...].astype(jnp.float32)).astype(jnp.bfloat16)
    left[2] = d_out.T
    pre_gate = dot_rows(token, ready(0))
    pre_up = dot_rows(token, ready(1))
    sig = jax.nn.sigmoid(pre_gate)
    silu = pre_gate * sig
    hidden[...] = (silu * pre_up).astype(jnp.bfloat16)
    d_hidden = jnp.dot(d_out, ready(2), preferred_element_type=jnp.float32)
    left[1] = (d_hidden * silu).astype(jnp.bfloat16).T
    left[0] = (d_hidden * pre_up * sig * (1.0 + pre_gate * (1.0 - sig))).astype(jnp.bfloat16).T

    def planes(fixed):
        return tuple(fixed.get(b, slice(None)) for b in reversed(range(bits)))

    free = min(3, bits)

    def order(p):
        return [(p + s) % free for s in range(free)] + list(range(free, bits))

    def chosen(p, steps):
        return {b: mine[b] for b in order(p)[:steps]}

    first, halvings = {}, {}

    def halve(p, s):
        b = order(p)[s]
        halvings[p, s] = remote(
            held.at[(p,) + planes({**chosen(p, s), b: 1 - mine[b]})],
            landing[s].at[p], r_send.at[p, s], r_recv.at[p, s], partners[b],
        )

    def gather_columns(p):
        for step in range(len(peers)):
            first[p, step].wait_recv()
        summed = grads[p, col].astype(jnp.float32)
        for step in range(len(peers)):
            summed = summed + from_col[step, p].astype(jnp.float32)
        for r in range(n_row):
            place_r = tuple((r >> b) & 1 for b in reversed(range(bits)))
            held[(p,) + place_r] = summed[r * unit : (r + 1) * unit, :].astype(jnp.bfloat16)
        halve(p, 0)

    joined = PART // WIDTH
    for start in range(0, parts, joined):
        for m, right in enumerate((keys, keys, hidden)):
            summed = jnp.dot(
                left[m], right[:, start * WIDTH : (start + joined) * WIDTH],
                preferred_element_type=jnp.float32,
            ).astype(jnp.bfloat16)
            for p in range(joined):
                for c in range(n_col):
                    grads[start + p, c, m * rows : (m + 1) * rows, :] = summed[
                        c * rows : (c + 1) * rows, p * WIDTH : (p + 1) * WIDTH
                    ]
        for p in range(start, start + joined):
            for step, peer in enumerate(peers):
                first[p, step] = remote(
                    grads.at[p, peer[1]], from_col.at[step, p],
                    c_send.at[p, step], c_recv.at[p, step], peer,
                )
        for p in range(start - joined, start):
            if p >= 0:
                gather_columns(p)
    for p in range(parts - joined, parts):
        gather_columns(p)
    for s in range(bits):
        for p in range(parts):
            halvings[p, s].wait_recv()
            index = (p,) + planes(chosen(p, s + 1))
            summed = held[index].astype(jnp.float32) + landing[s][p].astype(jnp.float32)
            if s < bits - 1:
                held[index] = summed.astype(jnp.bfloat16)
                halve(p, s + 1)
            else:
                total[:, p * WIDTH : (p + 1) * WIDTH] = summed

    if unit % 8 == 0:
        old = fast[pl.ds(pl.multiple_of(row * unit, 8), unit), :]
    else:
        old = sum(
            jnp.where(row == r, fast[r * unit : (r + 1) * unit, :], 0.0) for r in range(n_row)
        )
    moved = old - total[...]
    keep = jnp.sqrt(jnp.sum(old * old, axis=1, keepdims=True))
    new = moved * keep * lax.rsqrt(jnp.sum(moved * moved, axis=1, keepdims=True) + EPS_NORM)
    doublings, handed = {}, {}

    def double(p, s):
        part = (p, col) + planes(chosen(p, s + 1))
        doublings[p, s] = remote(
            out.at[part], out.at[part], g_send.at[p, s], g_recv.at[p, s], partners[order(p)[s]]
        )

    def hand(p, side, value):
        part = (p, col) + planes({order(p)[0]: value})
        for step, peer in enumerate(peers):
            handed[p, side, step] = remote(
                out.at[part], out.at[part], o_send.at[p, side, step], o_recv.at[p, side, step], peer
            )

    leaving = []

    def leave(p, step):
        giver = lax.rem(col + n_col - step, n_col)
        copy = pltpu.make_async_copy(out.at[p, giver], out_far.at[p, giver], x_sem.at[p, step])
        copy.start()
        leaving.append(copy)

    for p in range(parts):
        out[(p, col) + planes(chosen(p, bits))] = new[:, p * WIDTH : (p + 1) * WIDTH].astype(jnp.bfloat16)
        double(p, bits - 1)
    for s in reversed(range(bits)):
        for p in range(parts):
            doublings[p, s].wait_recv()
            if s > 0:
                double(p, s - 1)
            if s == 1:
                hand(p, 0, mine[order(p)[0]])
            if s == 0:
                hand(p, 1, 1 - mine[order(p)[0]])
                leave(p, 0)
    for p in range(parts):
        for step in range(len(peers)):
            for side in range(2):
                handed[p, side, step].wait_recv()
            leave(p, step + 1)
    for copy in edges.values():
        copy.wait_recv()
    for copy in leaving:
        copy.wait()
    for group in (given, edges, first, halvings, doublings, handed):
        for copy in group.values():
            copy.wait_send()


def update(n_row, n_col, gate, up, down, keys, values, queries, rates):
    rows, features = gate.shape
    tokens = keys.shape[0]
    parts = features // WIDTH
    stacked = 3 * rows
    bits = n_row.bit_length() - 1
    unit = stacked // n_row
    block = (2,) * bits + (unit, WIDTH)
    step = max(n_col - 1, 1)
    dma = pltpu.SemaphoreType.DMA
    landing = [VMEM((parts,) + (2,) * (bits - 1 - s) + (unit, WIDTH), jnp.bfloat16) for s in range(bits)]
    new, halo = pl.pallas_call(
        functools.partial(update_kernel, n_row, n_col, bits),
        out_shape=(
            jax.ShapeDtypeStruct((parts, n_col) + block, jnp.bfloat16),
            jax.ShapeDtypeStruct((2, tokens // 2, features), jnp.bfloat16),
        ),
        in_specs=[pl.BlockSpec(memory_space=pl.ANY)] * 6 + [pl.BlockSpec(memory_space=VMEM)],
        out_specs=(pl.BlockSpec(memory_space=pl.ANY), pl.BlockSpec(memory_space=pl.ANY)),
        scratch_shapes=[
            VMEM((parts, n_col) + block, jnp.bfloat16),
            VMEM((stacked, features), jnp.float32),
            VMEM((3, n_col, rows, features), jnp.bfloat16),
            VMEM((tokens, features), jnp.bfloat16),
            VMEM((tokens, features), jnp.bfloat16),
            VMEM((3, features, tokens), jnp.bfloat16),
            VMEM((tokens, features), jnp.bfloat16),
            VMEM((parts, n_col, stacked, WIDTH), jnp.bfloat16),
            VMEM((parts,) + block, jnp.bfloat16),
            VMEM((step, parts, stacked, WIDTH), jnp.bfloat16),
            *landing,
            VMEM((unit, features), jnp.float32),
            dma((3,)),
            dma((2,)),
            dma((parts, n_col)),
            dma((3, step)),
            dma((3, step)),
            dma((2,)),
            dma((2,)),
            dma((parts, step)),
            dma((parts, step)),
            dma((parts, bits)),
            dma((parts, bits)),
            dma((parts, bits)),
            dma((parts, bits)),
            dma((parts, 2, step)),
            dma((parts, 2, step)),
        ],
        compiler_params=pltpu.CompilerParams(
            collective_id=0, has_side_effects=True, vmem_limit_bytes=LIMIT
        ),
        cost_estimate=pl.CostEstimate(
            flops=12 * tokens * features * features, bytes_accessed=12 * 2**20, transcendentals=0
        ),
        name="update",
    )(gate, up, down, keys, values, queries, rates)
    return new.reshape(parts, n_col, stacked, WIDTH), halo


def attend_kernel(
    n_col, heads, temper, queries_in, halo_in, weights_in, gain, proj_q_in, proj_k_in, proj_v_in,
    attended, new_gate, new_up, new_down,
    queries, halo, weights, proj, wide, query_n, key_n, value_b, bias, in_sem, w_sem, p_sem, n_sem,
):
    rows = weights.shape[3]
    tokens, features = queries.shape
    parts = features // PART
    joined = PART // WIDTH
    half = tokens // 2
    size = features // heads
    col = lax.axis_index("col")
    proj_q, proj_k, proj_v = 0, 1, 2
    token_fills = [
        pltpu.make_async_copy(queries_in, queries, in_sem.at[0]),
        pltpu.make_async_copy(halo_in, halo, in_sem.at[1]),
    ]
    weight_fills = [
        pltpu.make_async_copy(
            weights_in.at[:, :, pl.ds(m * rows, rows), :], weights.at[m], w_sem.at[m]
        )
        for m in range(3)
    ]
    proj_fills = [
        pltpu.make_async_copy(source, proj.at[i], p_sem.at[i])
        for i, source in enumerate((proj_q_in, proj_k_in, proj_v_in))
    ]
    for fill in (
        token_fills[0], *weight_fills, proj_fills[1], proj_fills[2], proj_fills[0], token_fills[1]
    ):
        fill.start()
    stores = [
        pltpu.make_async_copy(wide.at[m], target, n_sem.at[m])
        for m, target in enumerate((new_gate, new_up, new_down))
    ]

    def whole(m, p):
        return jnp.concatenate(
            [
                jnp.concatenate([weights[m, p * joined + i, c] for i in range(joined)], axis=1)
                for c in range(n_col)
            ],
            axis=0,
        )

    def apply(m, left):
        return sum(dot_rows(left[:, p * PART : (p + 1) * PART], whole(m, p)) for p in range(parts))

    group_r = lax.broadcasted_iota(jnp.int32, (PART, PART), 0) // size
    group_c = lax.broadcasted_iota(jnp.int32, (PART, PART), 1) // size
    same = jnp.where(group_r == group_c, 1.0 / size, 0.0).astype(jnp.bfloat16)

    def head_norm(projected):
        pieces = []
        for p in range(parts):
            piece = projected[:, p * PART : (p + 1) * PART]
            square = piece * piece
            mean = jnp.dot(square.astype(jnp.bfloat16), same, preferred_element_type=jnp.float32)
            pieces.append((piece * lax.rsqrt(mean + EPS_NORM)).astype(jnp.bfloat16))
        return jnp.concatenate(pieces, axis=1)

    def project(normed, which):
        return jnp.dot(normed, proj[which], preferred_element_type=jnp.float32)

    at = lax.broadcasted_iota(jnp.int32, (half, half), 1) - lax.broadcasted_iota(
        jnp.int32, (half, half), 0
    )
    bias[0] = jnp.where(at >= 0, 0.0, -1e30)
    bias[1] = jnp.where(at <= 0, 0.0, -1e30)

    def arrive(fill, own):
        if own:
            fill.wait()

    for own in (True, False):
        token_fills[0 if own else 1].wait()
        tokens_in = queries[...] if own else jnp.concatenate([halo[0], halo[1]], axis=0)
        arrive(weight_fills[0], own)
        pre_gate = apply(0, tokens_in)
        arrive(weight_fills[1], own)
        pre_up = apply(1, tokens_in)
        mixed = (pre_gate * jax.nn.sigmoid(pre_gate) * pre_up).astype(jnp.bfloat16)
        arrive(weight_fills[2], own)
        fast_out = apply(2, mixed)
        inverse = lax.rsqrt(jnp.mean(fast_out * fast_out, axis=1, keepdims=True) + EPS_NORM)
        normed = (fast_out * inverse * gain[...][None, :]).astype(jnp.bfloat16)
        for fill in proj_fills:
            arrive(fill, own)
        keys = head_norm(project(normed, proj_k))
        values = project(normed, proj_v).astype(jnp.bfloat16)
        if own:
            query_n[...] = head_norm(project(normed, proj_q))
            key_n[half : half + tokens, :] = keys
            value_b[half : half + tokens, :] = values
        else:
            key_n[0:half, :] = keys[:half]
            value_b[0:half, :] = values[:half]
            key_n[half + tokens :, :] = keys[half:]
            value_b[half + tokens :, :] = values[half:]

    for m in range(3):
        for p in range(features // WIDTH):
            wide[m, :, p * WIDTH : (p + 1) * WIDTH] = weights[m, p, col].astype(jnp.float32)
        stores[m].start()
    pair = 128 // size
    lane = lax.broadcasted_iota(jnp.int32, (half, 128), 1) // size
    ones = jnp.ones((3 * half, 128), jnp.bfloat16)

    for j in range(features // 128):
        lanes = pl.ds(j * 128, 128)
        for block in range(2):
            span = pl.ds(block * half, half)
            window = pl.ds(block * half, 3 * half)
            query = query_n[span, lanes]
            key = key_n[window, lanes]
            value = jnp.concatenate([value_b[window, lanes], ones], axis=1)
            result = jnp.zeros((half, 128), jnp.float32)
            for h in range(pair):
                scale = temper[j * pair + h] * (math.log2(math.e) / math.sqrt(size))
                scores = dot_rows(jnp.where(lane == h, query, jnp.zeros_like(query)), key)
                scores = jnp.concatenate(
                    [
                        scores[:, :half] + bias[0],
                        scores[:, half : 2 * half],
                        scores[:, 2 * half :] + bias[1],
                    ],
                    axis=1,
                )
                highest = jnp.max(scores, axis=1, keepdims=True)
                weight = jnp.exp2((scores - highest) * scale).astype(jnp.bfloat16)
                both = jnp.dot(weight, value, preferred_element_type=jnp.float32)
                result = jnp.where(lane == h, both[:, :128] / both[:, 128:], result)
            attended[span, lanes] = result.astype(jnp.bfloat16)
    for store in stores:
        store.wait()


def attend(n_col, queries, halo, weights, gain, proj_q, proj_k, proj_v, temper):
    tokens, features = queries.shape
    rows = weights.shape[2] // 3
    half = tokens // 2
    vmem, far = pl.BlockSpec(memory_space=VMEM), pl.BlockSpec(memory_space=pl.ANY)
    square = jax.ShapeDtypeStruct((rows, features), jnp.float32)
    return pl.pallas_call(
        functools.partial(attend_kernel, n_col, temper.shape[0]),
        out_shape=(jax.ShapeDtypeStruct((tokens, features), jnp.bfloat16), square, square, square),
        in_specs=[pl.BlockSpec(memory_space=pltpu.SMEM), far, far, far, vmem, far, far, far],
        out_specs=(vmem, far, far, far),
        scratch_shapes=[
            VMEM((tokens, features), jnp.bfloat16),
            VMEM((2, half, features), jnp.bfloat16),
            VMEM((3, features // WIDTH, n_col, rows, WIDTH), jnp.bfloat16),
            VMEM((3, features, features), jnp.bfloat16),
            VMEM((3, rows, features), jnp.float32),
            VMEM((tokens, features), jnp.bfloat16),
            VMEM((2 * tokens, features), jnp.bfloat16),
            VMEM((2 * tokens, features), jnp.bfloat16),
            VMEM((2, half, half), jnp.float32),
            pltpu.SemaphoreType.DMA((2,)),
            pltpu.SemaphoreType.DMA((3,)),
            pltpu.SemaphoreType.DMA((3,)),
            pltpu.SemaphoreType.DMA((3,)),
        ],
        compiler_params=pltpu.CompilerParams(vmem_limit_bytes=LIMIT),
        name="attend",
    )(temper, queries, halo, weights, gain, proj_q, proj_k, proj_v)


def per_device(
    n_row,
    n_col,
    token_keys,
    token_values,
    token_queries,
    step_rates,
    fast_gate,
    fast_up,
    fast_down,
    norm_gain,
    proj_query,
    proj_key,
    proj_value,
    head_temper,
):
    new, halo = update(
        n_row, n_col, fast_gate, fast_up, fast_down,
        token_keys, token_values, token_queries, step_rates,
    )
    return attend(
        n_col, token_queries, halo, new, norm_gain, proj_query, proj_key, proj_value, head_temper
    )


def solution(mesh):
    placed = (
        P(("row", "col"), None),
        P(("row", "col"), None),
        P(("row", "col"), None),
        P(("row", "col")),
        P("col", None),
        P("col", None),
        P("col", None),
        P(),
        P(),
        P(),
        P(),
        P(),
    )
    return jax.shard_map(
        functools.partial(per_device, mesh.shape["row"], mesh.shape["col"]),
        mesh=mesh,
        in_specs=placed,
        out_specs=(P(("row", "col"), None), P("col", None), P("col", None), P("col", None)),
        check_vma=False,
    )
```

time: 108 us -> 79.6 us (0.74)
  Pallas kernels: 102 us -> 78.6 us
  local copies, waits for them, and re-layouts: 5.23 us -> 0 us
    pallas_call x2 -> x0, Pallas kernels: 23.5 us -> none  [the longest x1 15.3 us: exchange(): pl.pallas_call(functools.partial(exchange_kernel, n_row, n_col), out_shap...]
    unnamed x24 -> x0, local copies, waits for them, and re-layouts: 3.72 us -> none
    broadcast_in_dim x2 -> x0, local copies, waits for them, and re-layouts: 1.51 us -> none  [the longest x1 0.82 us: per_device(): step_rates[:, None]]
where the time goes in v2:
time: 79.6 us; the launch traced here: 79.4 us
  Pallas kernels  78.6 us (99%)
  between operations  0.8 us (1%)
    pallas_call x1, Pallas kernels, update(): pl.pallas_call(functools.partial(update_kernel, n_row, n_col, bits), out_...  56.3 us
    pallas_call x1, Pallas kernels, attend(): pl.pallas_call(functools.partial(attend_kernel, n_col, temper.shape[0]),...  22.3 us

profile of v2, /device:TPU:1, one launch (start us, length us, event | category | flops | bytes accessed | tf_op | source)
XLA Modules:
  0.0 79.4 jit_solution(894075973644994211)
XLA Ops:
  0.6 56.3 %update.1 = (bf16[6,2,2,2,2,2,72,128]{7,6,5,4,3,2,1,0:T(8,128)(2,1)}, bf16[2,256,768]{2,1,0:T(8,128)(2,1)}) custom-call(f32[384,768]{1,0:T(8,128)} %gate.1, f32[384,768]{1,0:T(8,128)} %up.1, f32[384,768]{1,0:T(8,128)} %down.1, bf16[512,768]{1,0:T(8,128)(2,1)} %keys_in.1, bf16[512,768]{1,0:T(8,128)(2,1)} %values_in.1, bf16[512,768]{1,0:T(8,128)(2,1)} %queries_in.1, ...), custom_call_target="tpu_custom_call" | custom-call | flops 3623878656 | bytes 12582912 | tf_op jit(solution)/shard_map/update/pallas_call | solution.py:255
  57.0 22.3 %attend.1 = (bf16[512,768]{1,0:T(8,128)(2,1)}, f32[384,768]{1,0:T(8,128)}, f32[384,768]{1,0:T(8,128)}, f32[384,768]{1,0:T(8,128)}) custom-call(f32[12]{0:T(128)} %temper.1, bf16[512,768]{1,0:T(8,128)(2,1)} %queries_in.1, bf16[2,256,768]{2,1,0:T(8,128)(2,1)} %get-tuple-element.6.halo_in, bf16[6,2,1152,128]{3,2,1,0:T(8,128)(2,1)} %bitcast.1, f32[768]{0:T(1024)} %gain.1, ...), custom_call_target="tpu_custom_call" | custom-call | tf_op jit(solution)/shard_map/attend/pallas_call | solution.py:446

commit v3 on v2

--- a/solution.py
+++ b/solution.py
@@ -13,6 +13,7 @@
 VMEM = pltpu.VMEM
 PART = 256
 WIDTH = 128
+ORDERS = ((1, 0, 3, 2), (3, 1, 2, 0), (0, 2, 1, 3), (0, 1, 2, 3), (1, 2, 3, 0), (2, 0, 1, 3))
 LIMIT = 60 * 1024 * 1024
 
 
@@ -123,6 +124,8 @@
     free = min(3, bits)
 
     def order(p):
+        if bits >= len(ORDERS[0]):
+            return list(ORDERS[p % len(ORDERS)]) + list(range(len(ORDERS[0]), bits))
         return [(p + s) % free for s in range(free)] + list(range(free, bits))
 
     def chosen(p, steps):
@@ -367,8 +370,8 @@
     at = lax.broadcasted_iota(jnp.int32, (half, half), 1) - lax.broadcasted_iota(
         jnp.int32, (half, half), 0
     )
-    bias[0] = jnp.where(at >= 0, 0.0, -1e30)
-    bias[1] = jnp.where(at <= 0, 0.0, -1e30)
+    bias[0] = jnp.where(at <= 0, 0.0, -1e30)
+    bias[1] = jnp.where(at >= 0, 0.0, -1e30)
 
     def arrive(fill, own):
         if own:
@@ -389,16 +392,16 @@
         for fill in proj_fills:
             arrive(fill, own)
         keys = head_norm(project(normed, proj_k))
-        values = project(normed, proj_v).astype(jnp.bfloat16)
+        values = project(normed, proj_v).astype(jnp.bfloat16).T
         if own:
             query_n[...] = head_norm(project(normed, proj_q))
             key_n[half : half + tokens, :] = keys
-            value_b[half : half + tokens, :] = values
+            value_b[:, half : half + tokens] = values
         else:
             key_n[0:half, :] = keys[:half]
-            value_b[0:half, :] = values[:half]
+            value_b[:, 0:half] = values[:, :half]
             key_n[half + tokens :, :] = keys[half:]
-            value_b[half + tokens :, :] = values[half:]
+            value_b[:, half + tokens :] = values[:, half:]
 
     for m in range(3):
         for p in range(features // WIDTH):
@@ -406,8 +409,7 @@
         stores[m].start()
     pair = 128 // size
     lane = lax.broadcasted_iota(jnp.int32, (half, 128), 1) // size
-    ones = jnp.ones((3 * half, 128), jnp.bfloat16)
-
+    ones = jnp.ones((16, 3 * half), jnp.bfloat16)
     for j in range(features // 128):
         lanes = pl.ds(j * 128, 128)
         for block in range(2):
@@ -415,24 +417,27 @@
             window = pl.ds(block * half, 3 * half)
             query = query_n[span, lanes]
             key = key_n[window, lanes]
-            value = jnp.concatenate([value_b[window, lanes], ones], axis=1)
-            result = jnp.zeros((half, 128), jnp.float32)
+            turned = []
             for h in range(pair):
-                scale = temper[j * pair + h] * (math.log2(math.e) / math.sqrt(size))
-                scores = dot_rows(jnp.where(lane == h, query, jnp.zeros_like(query)), key)
+                head = j * pair + h
+                scale = temper[head] * (math.log2(math.e) / math.sqrt(size))
+                scores = dot_rows(key, jnp.where(lane == h, query, jnp.zeros_like(query)))
                 scores = jnp.concatenate(
                     [
-                        scores[:, :half] + bias[0],
-                        scores[:, half : 2 * half],
-                        scores[:, 2 * half :] + bias[1],
+                        scores[:half] + bias[0],
+                        scores[half : 2 * half],
+                        scores[2 * half :] + bias[1],
                     ],
-                    axis=1,
+                    axis=0,
                 )
-                highest = jnp.max(scores, axis=1, keepdims=True)
+                highest = jnp.max(scores, axis=0, keepdims=True)
                 weight = jnp.exp2((scores - highest) * scale).astype(jnp.bfloat16)
-                both = jnp.dot(weight, value, preferred_element_type=jnp.float32)
-                result = jnp.where(lane == h, both[:, :128] / both[:, 128:], result)
-            attended[span, lanes] = result.astype(jnp.bfloat16)
+                value = jnp.concatenate(
+                    [value_b[head * size : (head + 1) * size, window], ones], axis=0
+                )
+                both = jnp.dot(value, weight, preferred_element_type=jnp.float32)
+                turned.append(both[:size] / both[size : size + 1])
+            attended[span, lanes] = jnp.concatenate(turned, axis=0).T.astype(jnp.bfloat16)
     for store in stores:
         store.wait()
 
@@ -456,7 +461,7 @@
             VMEM((3, rows, features), jnp.float32),
             VMEM((tokens, features), jnp.bfloat16),
             VMEM((2 * tokens, features), jnp.bfloat16),
-            VMEM((2 * tokens, features), jnp.bfloat16),
+            VMEM((features, 2 * tokens), jnp.bfloat16),
             VMEM((2, half, half), jnp.float32),
             pltpu.SemaphoreType.DMA((2,)),
             pltpu.SemaphoreType.DMA((3,)),

time: 79.6 us -> 87.2 us (1.095)
  Pallas kernels: 78.6 us -> 86.2 us
    pallas_call x1, Pallas kernels: 22.3 us -> 28.8 us  [attend(): pl.pallas_call(functools.partial(attend_kernel, n_col, temper.shape[0]),...]
    pallas_call x1, Pallas kernels: 56.3 us -> 57.4 us  [update(): pl.pallas_call(functools.partial(update_kernel, n_row, n_col, bits), out_...]
where the time goes in v3:
time: 87.2 us; the launch traced here: 87 us
  Pallas kernels  86.2 us (99%)
    pallas_call x1, Pallas kernels, update(): pl.pallas_call(functools.partial(update_kernel, n_row, n_col, bits), out_...  57.4 us
    pallas_call x1, Pallas kernels, attend(): pl.pallas_call(functools.partial(attend_kernel, n_col, temper.shape[0]),...  28.8 us

profile of v3, /device:TPU:1, one launch (start us, length us, event | category | flops | bytes accessed | tf_op | source)
XLA Modules:
  0.0 87.0 jit_solution(10379099462052959682)
XLA Ops:
  0.6 57.4 %update.1 = (bf16[6,2,2,2,2,2,72,128]{7,6,5,4,3,2,1,0:T(8,128)(2,1)}, bf16[2,256,768]{2,1,0:T(8,128)(2,1)}) custom-call(f32[384,768]{1,0:T(8,128)} %gate.1, f32[384,768]{1,0:T(8,128)} %up.1, f32[384,768]{1,0:T(8,128)} %down.1, bf16[512,768]{1,0:T(8,128)(2,1)} %keys_in.1, bf16[512,768]{1,0:T(8,128)(2,1)} %values_in.1, bf16[512,768]{1,0:T(8,128)(2,1)} %queries_in.1, ...), custom_call_target="tpu_custom_call" | custom-call | flops 3623878656 | bytes 12582912 | tf_op jit(solution)/shard_map/update/pallas_call | solution.py:258
  58.0 28.8 %attend.1 = (bf16[512,768]{1,0:T(8,128)(2,1)}, f32[384,768]{1,0:T(8,128)}, f32[384,768]{1,0:T(8,128)}, f32[384,768]{1,0:T(8,128)}) custom-call(f32[12]{0:T(128)} %temper.1, bf16[512,768]{1,0:T(8,128)(2,1)} %queries_in.1, bf16[2,256,768]{2,1,0:T(8,128)(2,1)} %get-tuple-element.6.halo_in, bf16[6,2,1152,128]{3,2,1,0:T(8,128)(2,1)} %bitcast.1, f32[768]{0:T(1024)} %gain.1, ...), custom_call_target="tpu_custom_call" | custom-call | tf_op jit(solution)/shard_map/attend/pallas_call | solution.py:451

commit v4 on v2

--- a/solution.py
+++ b/solution.py
@@ -408,31 +408,49 @@
     lane = lax.broadcasted_iota(jnp.int32, (half, 128), 1) // size
     ones = jnp.ones((3 * half, 128), jnp.bfloat16)
 
-    for j in range(features // 128):
+    tasks = [(j, block) for j in range(features // 128) for block in range(2)]
+
+    def score(j, block):
         lanes = pl.ds(j * 128, 128)
-        for block in range(2):
-            span = pl.ds(block * half, half)
-            window = pl.ds(block * half, 3 * half)
-            query = query_n[span, lanes]
-            key = key_n[window, lanes]
-            value = jnp.concatenate([value_b[window, lanes], ones], axis=1)
-            result = jnp.zeros((half, 128), jnp.float32)
-            for h in range(pair):
-                scale = temper[j * pair + h] * (math.log2(math.e) / math.sqrt(size))
-                scores = dot_rows(jnp.where(lane == h, query, jnp.zeros_like(query)), key)
-                scores = jnp.concatenate(
-                    [
-                        scores[:, :half] + bias[0],
-                        scores[:, half : 2 * half],
-                        scores[:, 2 * half :] + bias[1],
-                    ],
-                    axis=1,
-                )
-                highest = jnp.max(scores, axis=1, keepdims=True)
-                weight = jnp.exp2((scores - highest) * scale).astype(jnp.bfloat16)
-                both = jnp.dot(weight, value, preferred_element_type=jnp.float32)
-                result = jnp.where(lane == h, both[:, :128] / both[:, 128:], result)
-            attended[span, lanes] = result.astype(jnp.bfloat16)
+        query = query_n[pl.ds(block * half, half), lanes]
+        stacked = jnp.concatenate(
+            [jnp.where(lane == h, query, jnp.zeros_like(query)) for h in range(pair)], axis=0
+        )
+        return dot_rows(stacked, key_n[pl.ds(block * half, 3 * half), lanes])
+
+    def soften(j, scores):
+        weights_b = []
+        for h in range(pair):
+            scale = temper[j * pair + h] * (math.log2(math.e) / math.sqrt(size))
+            mine = scores[h * half : (h + 1) * half]
+            mine = jnp.concatenate(
+                [
+                    mine[:, :half] + bias[0],
+                    mine[:, half : 2 * half],
+                    mine[:, 2 * half :] + bias[1],
+                ],
+                axis=1,
+            )
+            highest = jnp.max(mine, axis=1, keepdims=True)
+            weights_b.append(jnp.exp2((mine - highest) * scale).astype(jnp.bfloat16))
+        return jnp.concatenate(weights_b, axis=0)
+
+    def finish(j, block, weight):
+        lanes = pl.ds(j * 128, 128)
+        value = jnp.concatenate([value_b[pl.ds(block * half, 3 * half), lanes], ones], axis=1)
+        both = jnp.dot(weight, value, preferred_element_type=jnp.float32)
+        result = jnp.zeros((half, 128), jnp.float32)
+        for h in range(pair):
+            mine = both[h * half : (h + 1) * half]
+            result = jnp.where(lane == h, mine[:, :128] / mine[:, 128:], result)
+        attended[pl.ds(block * half, half), lanes] = result.astype(jnp.bfloat16)
+
+    ahead = score(*tasks[0])
+    for i, (j, block) in enumerate(tasks):
+        scores = ahead
+        if i + 1 < len(tasks):
+            ahead = score(*tasks[i + 1])
+        finish(j, block, soften(j, scores))
     for store in stores:
         store.wait()
 

time: 79.6 us -> 79.5 us (level)
  no operation moved by 1% of the time
where the time goes in v4:
time: 79.5 us; the launch traced here: 79.3 us
  Pallas kernels  78.5 us (99%)
  between operations  0.8 us (1%)
    pallas_call x1, Pallas kernels, update(): pl.pallas_call(functools.partial(update_kernel, n_row, n_col, bits), out_...  56.3 us
    pallas_call x1, Pallas kernels, attend(): pl.pallas_call(functools.partial(attend_kernel, n_col, temper.shape[0]),...  22.2 us

profile of v4, /device:TPU:1, one launch (start us, length us, event | category | flops | bytes accessed | tf_op | source)
XLA Modules:
  0.0 79.3 jit_solution(784954293225770115)
XLA Ops:
  0.6 56.3 %update.1 = (bf16[6,2,2,2,2,2,72,128]{7,6,5,4,3,2,1,0:T(8,128)(2,1)}, bf16[2,256,768]{2,1,0:T(8,128)(2,1)}) custom-call(f32[384,768]{1,0:T(8,128)} %gate.1, f32[384,768]{1,0:T(8,128)} %up.1, f32[384,768]{1,0:T(8,128)} %down.1, bf16[512,768]{1,0:T(8,128)(2,1)} %keys_in.1, bf16[512,768]{1,0:T(8,128)(2,1)} %values_in.1, bf16[512,768]{1,0:T(8,128)(2,1)} %queries_in.1, ...), custom_call_target="tpu_custom_call" | custom-call | flops 3623878656 | bytes 12582912 | tf_op jit(solution)/shard_map/update/pallas_call | solution.py:255
  57.0 22.2 %attend.1 = (bf16[512,768]{1,0:T(8,128)(2,1)}, f32[384,768]{1,0:T(8,128)}, f32[384,768]{1,0:T(8,128)}, f32[384,768]{1,0:T(8,128)}) custom-call(f32[12]{0:T(128)} %temper.1, bf16[512,768]{1,0:T(8,128)(2,1)} %queries_in.1, bf16[2,256,768]{2,1,0:T(8,128)(2,1)} %get-tuple-element.6.halo_in, bf16[6,2,1152,128]{3,2,1,0:T(8,128)(2,1)} %bitcast.1, f32[768]{0:T(1024)} %gain.1, ...), custom_call_target="tpu_custom_call" | custom-call | tf_op jit(solution)/shard_map/attend/pallas_call | solution.py:464
